TPU v7x, 32 devices: a whole 2x2x4 slice. The times are simulated.
32 devices in a mesh: dp: 4 (over x, core), tm: 8 (over z, y).
Axes of the slice: x: 2, y: 2, z: 4, core: 2. Of those that a mesh axis runs over, the one named last changes fastest.
Arguments:
- tokens: bfloat16 [4, 8, 512, 768], P('dp', 'tm'), may hold values from -60 to 60
- qkv_weight: bfloat16 [768, 2304], replicated, may hold values from -0.21875 to 0.21875
- pool_kernel: float32 [2, 27, 64], replicated, may hold values from -1.25 to 1.25
- norm_gain: float32 [2, 64], replicated, may hold values from 0.1 to 1.9
- out_weight: bfloat16 [768, 768], replicated, may hold values from -0.21875 to 0.21875
- out_cotangent: bfloat16 [4, 8, 512, 768], P('dp', 'tm'), may hold values from -6 to 6
Outputs:
- block_out: bfloat16 [4, 8, 512, 768], P('dp', 'tm')
- grad_tokens: bfloat16 [4, 8, 512, 768], P('dp', 'tm')
- grad_qkv_weight: float32 [768, 2304], P('tm')
- grad_out_weight: float32 [768, 768], P('tm')
- grad_kernel: float32 [2, 27, 64], replicated
- grad_gain: float32 [2, 64], replicated
All inputs are finite; a program needn't handle non-finite values.
Results may differ from a plain program's by a relative error of at most 0.0055.
The roundings to bfloat16 on the way count: a program that leaves them out, or rounds other values in their place, can miss the bound.
Values may be sent and summed in bfloat16 or wider, within the bound.
A program may use at most 128 MiB of HBM per device.

v0:
```python
from functools import partial

import jax
import jax.numpy as jnp
from jax import lax
from jax.sharding import PartitionSpec as P

HEADS = 12
GRID_H = 32


EPSILON = 1e-05
pair_heads = 2


def shifted_2(value, axis, steps):
    count = lax.axis_size(axis)
    first, last = (max(0, -steps), min(count, count - steps))
    return lax.ppermute(value, axis, [(source, source + steps) for source in range(first, last)])


def extended(array, sides, width):
    for axis, dim in sides:
        size, length = (lax.axis_size(axis), array.shape[dim])
        up = [(i, (i + 1) % size) for i in range(size - 1)]
        down = [(j, i) for i, j in up]
        last = lax.slice_in_dim(array, length - width, length, axis=dim)
        first = lax.slice_in_dim(array, 0, width, axis=dim)
        before = lax.ppermute(last, axis, up)
        after = lax.ppermute(first, axis, down)
        array = jnp.concatenate([before, array, after], axis=dim)
    return array


def tap_table(kernel, head_count):
    tiled = jnp.tile(kernel, (1, 1, head_count))
    return jnp.transpose(tiled, (1, 0, 2)).reshape(3, 3, 3, -1)


def cut_blocks(volume):
    lead_dims = volume.ndim - 3
    extent = volume.shape
    padded = jnp.pad(volume, [(0, 0)] * lead_dims + [(1, 3), (1, 3), (0, 0)])
    pooled_h = extent[-3] // 4
    pooled_w = extent[-2] // 4
    tiled_view = padded.reshape(extent[:-3] + (pooled_h + 1, 4, pooled_w + 1, 4, extent[-1]))
    return tiled_view[..., :pooled_h, :3, :pooled_w, :3, :]


def spatial_sums(blocks, kernel_taps):
    widened = blocks.astype(jnp.float32)
    results = []
    for offset_t in range(3):
        running = None
        for offset_h in range(3):
            for offset_w in range(3):
                product_term = (
                    widened[..., offset_h, :, offset_w, :]
                    * kernel_taps[offset_t, offset_h, offset_w]
                )
                running = product_term if running is None else running + product_term
        results.append(running)
    return results


def spread_taps(shifted, kernel_taps, height, breadth):
    running = None
    for offset_t in range(3):
        product_term = (
            shifted[offset_t][..., :, None, :, None, :] * kernel_taps[offset_t][:, None, :, :]
        )
        running = product_term if running is None else running + product_term
    lead_dims = running.ndim - 5
    padded = jnp.pad(running, [(0, 0)] * lead_dims + [(0, 1)] * 4 + [(0, 0)])
    extent = padded.shape
    volume = padded.reshape(
        extent[:lead_dims] + (extent[lead_dims] * 4, extent[lead_dims + 2] * 4, extent[-1])
    )
    return volume[..., 1 : height + 1, 1 : breadth + 1, :]


def tap_grads(shifted, blocks, head_count):
    widened = blocks.astype(jnp.float32)
    per_offset = [
        jnp.einsum(
            "cfijd,cfibjed->bed", shifted[offset_t], widened, precision=lax.Precision.HIGHEST
        )
        for offset_t in range(3)
    ]
    stacked = jnp.stack(per_offset).reshape(27, 2, head_count, -1)
    return jnp.transpose(jnp.sum(stacked, axis=2), (1, 0, 2))


def pooled_norm(summed, gain, head_count):
    grouped_view = summed.reshape(summed.shape[:-1] + (2, head_count, -1))
    centred = grouped_view - jnp.mean(grouped_view, axis=-1, keepdims=True)
    inv_std = lax.rsqrt(jnp.mean(centred * centred, axis=-1, keepdims=True) + EPSILON)
    normed = centred * inv_std
    pooled = (normed * gain[:, None, :]).reshape(summed.shape).astype(jnp.bfloat16)
    return (pooled, normed, inv_std)


def split_heads(tensor):
    extent = tensor.shape
    paired = tensor.reshape(extent[:2] + (extent[2] // pair_heads, pair_heads) + extent[3:])
    return jnp.moveaxis(paired, 2, 0)


def join_heads(tensor):
    moved = jnp.moveaxis(tensor, 0, 2)
    extent = moved.shape
    return moved.reshape(extent[:2] + (extent[2] * extent[3],) + extent[4:])


def by_pairs(function, tensors):
    results = lax.map(
        lambda members: function(*members), tuple((split_heads(element) for element in tensors))
    )
    return tuple((join_heads(element) for element in results))


def group_forward(queries, keys_part, values_part, softmax_scale):
    scores = (
        jnp.einsum("crgd,ckgd->crgk", queries, keys_part, preferred_element_type=jnp.float32)
        * softmax_scale
    )
    row_max = jnp.max(scores, axis=-1)
    weights = jnp.exp(scores - row_max[..., None])
    row_total = jnp.sum(weights, axis=-1)
    weighted = jnp.einsum(
        "crgk,ckgd->crgd",
        weights.astype(jnp.bfloat16),
        values_part,
        preferred_element_type=jnp.float32,
    )
    return (row_max, row_total, weighted)


def group_backward(
    queries, keys_part, values_part, row_max, row_total, attended, d_mixed, softmax_scale
):
    scores = (
        jnp.einsum("crgd,ckgd->crgk", queries, keys_part, preferred_element_type=jnp.float32)
        * softmax_scale
    )
    weights = jnp.exp(scores - row_max[..., None])
    probability = weights / row_total[..., None]
    d_widened = d_mixed.astype(jnp.float32)
    scaled_grad = (d_widened / row_total[..., None]).astype(jnp.bfloat16)
    d_values = jnp.einsum(
        "crgk,crgd->ckgd",
        weights.astype(jnp.bfloat16),
        scaled_grad,
        preferred_element_type=jnp.float32,
    )
    d_probs = jnp.einsum(
        "crgd,ckgd->crgk", d_mixed, values_part, preferred_element_type=jnp.float32
    )
    row_delta = jnp.sum(d_widened * attended, axis=-1)
    d_scores = (probability * (d_probs - row_delta[..., None])).astype(jnp.bfloat16)
    d_queries = (
        jnp.einsum("crgk,ckgd->crgd", d_scores, keys_part, preferred_element_type=jnp.float32)
        * softmax_scale
        + d_widened
    )
    d_keys = (
        jnp.einsum("crgk,crgd->ckgd", d_scores, queries, preferred_element_type=jnp.float32)
        * softmax_scale
    )
    return (d_queries, d_keys, d_values)


def shards(tokens, qkv_weight, pool_kernel, norm_gain, out_weight, out_cotangent):
    clip_count, frame_count, cell_count, model_width = tokens.shape
    head_count = HEADS
    head_size = model_width // head_count
    softmax_scale = head_size ** (-0.5)
    query_rows = frame_count * cell_count
    breadth = cell_count // GRID_H
    token_rows = tokens.reshape(-1, model_width)
    projected = jnp.dot(token_rows, qkv_weight, preferred_element_type=jnp.float32).astype(
        jnp.bfloat16
    )
    projected = projected.reshape(clip_count, frame_count, cell_count, 3 * model_width)
    queries = projected[..., :model_width].reshape(clip_count, query_rows, head_count, head_size)
    volume = projected[..., model_width:].reshape(
        clip_count, frame_count, GRID_H, breadth, 2 * model_width
    )
    kernel_taps = tap_table(pool_kernel, head_count)
    own_blocks = cut_blocks(volume)
    partials = spatial_sums(own_blocks, kernel_taps)
    from_lower = shifted_2(partials[0], "tm", 1)
    from_upper = shifted_2(partials[2], "tm", -1)
    pooled_sum = (
        jnp.concatenate([from_lower, partials[0][:, : frame_count - 1]], axis=1)
        + partials[1]
        + jnp.concatenate([partials[2][:, 1:], from_upper], axis=1)
    )
    pooled, normed, inv_std = pooled_norm(pooled_sum, norm_gain, head_count)
    pooled = pooled.reshape(clip_count, -1, 2 * model_width)
    gathered = lax.all_gather(pooled, "tm", axis=1, tiled=True)
    keys_part = gathered[..., :model_width].reshape(clip_count, -1, head_count, head_size)
    values_part = gathered[..., model_width:].reshape(clip_count, -1, head_count, head_size)
    row_max, row_total, weighted = by_pairs(
        partial(group_forward, softmax_scale=softmax_scale), (queries, keys_part, values_part)
    )
    attended = weighted / row_total[..., None]
    mixed = (attended + queries.astype(jnp.float32)).astype(jnp.bfloat16)
    mixed_rows = mixed.reshape(-1, model_width)
    block_out = (
        jnp.dot(mixed_rows, out_weight, preferred_element_type=jnp.float32)
        .astype(jnp.bfloat16)
        .reshape(tokens.shape)
    )
    cotangent_rows = out_cotangent.reshape(-1, model_width)
    d_mixed = jnp.einsum(
        "re,de->rd", cotangent_rows, out_weight, preferred_element_type=jnp.float32
    ).astype(jnp.bfloat16)
    d_mixed = d_mixed.reshape(clip_count, query_rows, head_count, head_size)
    out_local = jnp.einsum(
        "rd,re->de", mixed_rows, cotangent_rows, preferred_element_type=jnp.float32
    )
    keys_all = gathered[..., :model_width].reshape(clip_count, -1, head_count, head_size)
    values_all = gathered[..., model_width:].reshape(clip_count, -1, head_count, head_size)
    d_queries, d_keys, d_values = by_pairs(
        partial(group_backward, softmax_scale=softmax_scale),
        (queries, keys_all, values_all, row_max, row_total, attended, d_mixed),
    )
    d_pooled_all = jnp.concatenate(
        [
            d_keys.reshape(clip_count, -1, model_width),
            d_values.reshape(clip_count, -1, model_width),
        ],
        axis=-1,
    )
    d_pooled = lax.psum_scatter(d_pooled_all, "tm", scatter_dimension=1, tiled=True)
    d_grouped = d_pooled.reshape(normed.shape)
    sum_axes = tuple(range(normed.ndim - 3)) + (normed.ndim - 2,)
    gain_local = jnp.sum(d_grouped * normed, axis=sum_axes)
    d_normed = d_grouped * norm_gain[:, None, :]
    d_summed = inv_std * (
        d_normed
        - jnp.mean(d_normed, axis=-1, keepdims=True)
        - normed * jnp.mean(d_normed * normed, axis=-1, keepdims=True)
    )
    d_summed = d_summed.reshape(pooled_sum.shape)
    rims = extended(d_summed, (("tm", 1),), 1)
    shifted = [rims[:, 2:], rims[:, 1 : frame_count + 1], rims[:, :frame_count]]
    d_volume = spread_taps(shifted, kernel_taps, GRID_H, breadth)
    kernel_local = tap_grads(shifted, own_blocks, head_count)
    d_projected = jnp.concatenate(
        [
            d_queries.reshape(clip_count, frame_count, cell_count, model_width),
            d_volume.reshape(clip_count, frame_count, cell_count, 2 * model_width),
        ],
        axis=-1,
    )
    d_projected = d_projected.astype(jnp.bfloat16).reshape(-1, 3 * model_width)
    grad_tokens = (
        jnp.einsum("re,de->rd", d_projected, qkv_weight, preferred_element_type=jnp.float32)
        .astype(jnp.bfloat16)
        .reshape(tokens.shape)
    )
    qkv_local = jnp.einsum("rd,re->de", token_rows, d_projected, preferred_element_type=jnp.float32)
    norm_scale = float(
        clip_count * frame_count * cell_count * lax.axis_size("dp") * lax.axis_size("tm")
    ) ** (-0.5)
    partial_qkv, partial_out = (
        lax.psum_scatter(qkv_local, "tm", scatter_dimension=0, tiled=True),
        lax.psum_scatter(out_local, "tm", scatter_dimension=0, tiled=True),
    )
    shard_qkv, shard_out = lax.psum((partial_qkv, partial_out), "dp")
    kernel_total, gain_total = lax.psum((kernel_local, gain_local), ("dp", "tm"))
    return (
        block_out,
        grad_tokens,
        shard_qkv * norm_scale,
        shard_out * norm_scale,
        kernel_total * norm_scale,
        gain_total * norm_scale,
    )


def solution(mesh):
    placed = (P("dp", "tm", None, None), P(), P(), P(), P(), P("dp", "tm", None, None))
    return jax.shard_map(
        shards,
        mesh=mesh,
        in_specs=placed,
        out_specs=(
            P("dp", "tm", None, None),
            P("dp", "tm", None, None),
            P("tm", None),
            P("tm", None),
            P(),
            P(),
        ),
        check_vma=False,
    )
```

profile of v0, /device:TPU:0, one launch (start us, length us, event | category | flops | bytes accessed | tf_op | source)
XLA Modules:
  0.0 601.5 jit_solution(6102147583223295620)
XLA Ops:
  8.9 1.9 tile.10
  12.5 2.0 slice_reduce_fusion.17
  14.5 3.1 fusion.52
  19.9 1.9 pad.9
  21.9 4.2 reshape.1034
  26.1 1.9 slice.205
  33.3 6.2 %collective-permute-start = (f32[1,1,8,4,1536]{4,2,3,1,0:T(8,128)}, f32[1,1,8,4,1536]{4,2,3,1,0:T(8,128)}, u32[]{:S(2)}, u32[]{:S(2)}) collective-permute-start(f32[1,1,8,4,1536]{4,2,3,1,0:T(8,128)} %multiply_add_fusion.1), channel_id=1, source_target_pairs={{0,1},{1,2},{2,3},{3,4},{4,5},{5,6},{6,7},{8,9},{9,10},{10,11},{11... | collective-permute-start | bytes 589832 | tf_op jit(solution)/shard_map/ppermute | solution.py:19
  41.1 2.1 slice.243
  44.6 2.4 copy.269
  47.0 2.3 copy.261
  50.2 2.5 add_add_fusion
  52.7 1.9 reshape.1037
  54.6 1.9 reshape.1036
  56.5 1.9 reduce_sum.79
  63.4 1.9 reshape.1060
  67.1 1.9 reshape.1061
  72.5 33.1 %all_gather.3 = bf16[1,256,1536]{2,1,0:T(8,128)(2,1)S(1)} all-gather(bf16[1,32,1536]{2,1,0:T(8,128)(2,1)} %reshape.1038), channel_id=1, replica_groups=mesh['dp'=4,'tm'=8] {'tm'}, dimensions={1}, use_global_device_ids=true | all-gather | bytes 884736 | tf_op jit(solution)/shard_map/all_gather | solution.py:201
  106.5 1.9 copy.262
  108.4 1.9 copy.260
  110.3 23.5 %while.30 = (s32[]{:T(128)}, f32[6,1,512,2]{2,3,1,0:T(2,128)}, f32[6,1,512,2]{2,3,1,0:T(2,128)}, f32[6,1,512,2,64]{2,4,3,1,0:T(8,128)}, bf16[6,1,256,2,64]{2,4,3...) while((s32[]{:T(128)}, f32[6,1,512,2]{2,3,1,0:T(2,128)}, ...), condition=%wide.region_5.6_spmd.clone, body=%wide.region_2.5_spmd.sunk.clone | while | flops 68679680 | bytes 3704921 | solution.py:116
  132.0 1.9 fusion.140
  133.8 2.8 broadcast_divide_fusion
  136.6 52.8 %while.31 = (s32[]{:T(128)}, bf16[6,1,512,2,64]{2,4,3,1,0:T(8,128)(2,1)}, f32[6,1,256,2,64]{2,4,3,1,0:T(8,128)}, f32[6,1,256,2,64]{2,4,3,1,0:T(8,128)}, bf16[6,1...) while((s32[]{:T(128)}, ...), condition=%wide.region_8.9_spmd.clone, body=%wide.region_6.8_spmd.sunk.clone | while | flops 170228736 | bytes 9675929 | solution.py:116
  150.6 1.8 fusion.154
  168.2 1.8 fusion.154
  185.8 1.8 fusion.154
  189.3 2.6 pad_maximum_fusion.1
  192.0 4.9 copy.277
  209.4 1.9 reshape.1063
  211.4 1.9 reshape.1062
  213.3 2.3 copy.287
  215.6 69.5 %all-reduce.8.cloned.1.call-done = f32[1,256,1536]{2,0,1:T(1,128)} async-done(((f32[1,256,1536]{2,0,1:T(1,128)}), f32[1,256,1536]{2,0,1:T(1,128)}) %all-reduce.8.cloned.1.call-update) | async-done | bytes 1572880
  285.1 2.5 fusion.85
  289.2 1.9 reshape.1043
  291.1 1.9 multiply_reduce_fusion
  294.6 1.9 mul.921
  296.5 1.9 mul.909
  300.1 1.9 sub.131
  302.0 1.9 sub.128
  305.4 3.4 collective-permute-start.3
  311.7 5.7 collective-permute-done.3
  319.1 2.1 pad.10
  321.1 4.1 reshape.1046
  325.2 2.0 slice.248
  329.3 5.0 convolution_bitcast_fusion.3
  334.3 8.0 %copy.318 = f32[768,2304]{1,0:T(8,128)} copy(f32[768,2304]{0,1:T(8,128)} %convolution_bitcast_fusion.3) | data formatting | bytes 14155776
  342.4 2.0 fusion.58
  344.4 2.2 fusion.65
  348.7 1.9 sub.136
  350.6 1.9 mul.939
  353.9 2.1 div.67
  355.9 3.1 copy.268
  359.0 3.0 copy.267
  362.0 4.2 fusion.62
  368.3 2.2 fusion.53
  371.2 1.9 reshape.1050
  374.9 45.0 %all-reduce.3 = (f32[2,27,64]{2,0,1:T(2,128)}, f32[2,64]{1,0:T(2,128)S(1)}) all-reduce(f32[2,27,64]{2,0,1:T(2,128)} %bitcast.464, f32[2,64]{1,0:T(2,128)S(1)} %copy-done.30), channel_id=1, replica_groups=mesh['dp'=4,'tm'=8] {'dp','tm'}, use_global_device_ids=true, to_apply=%region_17.18 | all-reduce | flops 3584 | bytes 28672 | tf_op jit(solution)/shard_map/psum | solution.py:273
  421.3 52.0 %reduce-scatter.7.cloned.1.call-done = f32[96,2304]{1,0:T(8,128)} async-done(((f32[768,2304]{1,0:T(8,128)}), f32[96,2304]{1,0:T(8,128)}) %reduce-scatter.7.cloned.1.call-update) | async-done | bytes 884752
  473.2 2.5 copy.319
  475.8 69.6 %reduce-scatter.5.cloned.1.call-done = f32[96,768]{1,0:T(8,128)} async-done(((f32[768,768]{1,0:T(8,128)}), f32[96,768]{1,0:T(8,128)}) %reduce-scatter.5.cloned.1.call-update) | async-done | bytes 294928 | tf_op jit(solution)/shard_map/reduce_scatter | solution.py:270
  545.9 4.5 fusion.61
  550.4 37.9 %all-reduce.10.cloned.1.call-done = (f32[96,2304]{0,1:T(8,128)}, f32[96,768]{1,0:T(8,128)}) async-done(((f32[96,2304]{0,1:T(8,128)}, f32[96,768]{1,0:T(8,128)}), (f32[96,2304]{0,1:T(8,128)}, f32[96,768]{1,0:T(8,128)})) %all-reduce.10.cloned.1.call-update) | async-done | bytes 1179664 | tf_op jit(solution)/shard_map/psum | solution.py:272
  588.3 2.4 broadcast_multiply_fusion
  590.7 2.5 copy.291
  (211 shorter events, 131.5 us)
Async XLA Ops:
  7.2 7.4 %copy-start = (bf16[768,2304]{1,0:T(8,128)(2,1)S(1)}, bf16[768,2304]{1,0:T(8,128)(2,1)}, u32[]{:S(2)}) copy-start(bf16[768,2304]{1,0:T(8,128)(2,1)} %param.11) | copy-start | bytes 10616836
  7.2 277.9 %all-reduce.8.cloned.1.call-start = ((), (), s32[]{:S(2)}) async-start(), calls=%async_computation.4 | async-start | bytes 3145728
  17.7 1.4 copy-start.4
  28.0 2.0 copy-start.2
  28.0 0.7 copy-start.21
  28.0 0.8 copy-start.22
  28.0 0.8 copy-start.23
  28.0 0.9 copy-start.24
  28.0 0.9 copy-start.25
  28.1 0.9 copy-start.26
  28.1 1.0 copy-start.27
  28.1 1.0 copy-start.28
  28.1 1.1 copy-start.29
  28.4 4.9 copy-start.1
  30.0 9.4 %copy-start.11 = (bf16[1,1,512,768]{3,2,1,0:T(8,128)(2,1)S(1)}, bf16[1,1,512,768]{3,2,1,0:T(8,128)(2,1)}, u32[]{:S(2)}) copy-start(bf16[1,1,512,768]{3,2,1,0:T(8,128)(2,1)} %param.15) | copy-start | bytes 2359300
  30.0 9.4 %copy-start.33 = (bf16[768,768]{1,0:T(8,128)(2,1)S(1)}, bf16[768,768]{1,0:T(8,128)(2,1)}, u32[]{:S(2)}) copy-start(bf16[768,768]{1,0:T(8,128)(2,1)} %param.14) | copy-start | bytes 3538948
  30.0 20.2 %collective-permute-start.1 = (f32[1,1,8,4,1536]{4,2,3,1,0:T(8,128)}, f32[1,1,8,4,1536]{4,2,3,1,0:T(8,128)}, u32[]{:S(2)}, u32[]{:S(2)}) collective-permute-start(f32[1,1,8,4,1536]{4,2,3,1,0:T(8,128)} %multiply_add_fusion), channel_id=1, source_target_pairs={{1,0},{2,1},{3,2},{4,3},{5,4},{6,5},{7,6},{9,8},{10,9},{11,10},{12... | collective-permute-start | bytes 589832 | tf_op jit(solution)/shard_map/ppermute | solution.py:19
  33.3 16.9 %collective-permute-start = (f32[1,1,8,4,1536]{4,2,3,1,0:T(8,128)}, f32[1,1,8,4,1536]{4,2,3,1,0:T(8,128)}, u32[]{:S(2)}, u32[]{:S(2)}) collective-permute-start(f32[1,1,8,4,1536]{4,2,3,1,0:T(8,128)} %multiply_add_fusion.1), channel_id=1, source_target_pairs={{0,1},{1,2},{2,3},{3,4},{4,5},{5,6},{6,7},{8,9},{9,10},{10,11},{11... | collective-permute-start | bytes 589832 | tf_op jit(solution)/shard_map/ppermute | solution.py:19
  41.1 2.1 copy-start.31
  59.1 0.6 copy-start.16
  61.2 0.6 copy-start.20
  136.6 3.1 copy-start.3
  145.4 3.1 copy-start.3
  154.2 3.1 copy-start.3
  163.0 3.1 copy-start.3
  171.8 3.1 copy-start.3
  180.5 3.1 copy-start.3
  196.8 0.7 copy-start.35
  196.9 276.4 %reduce-scatter.7.cloned.1.call-start = ((), (), s32[]{:S(2)}) async-start(), calls=%async_computation.3 | async-start | bytes 7962624
  213.3 77.8 %copy-start.32 = (f32[2,64]{1,0:T(2,128)S(1)}, f32[2,64]{1,0:T(2,128)}, u32[]{:S(2)}) copy-start(f32[2,64]{1,0:T(2,128)} %param.13) | copy-start | bytes 1540
  303.8 14.3 %copy-start.17 = (f32[3,3,1536]{2,0,1:T(4,128)S(1)}, f32[3,3,1536]{2,0,1:T(4,128)}, u32[]{:S(2)}) copy-start(f32[3,3,1536]{2,0,1:T(4,128)} %copy.280) | copy-start | bytes 165892
  303.8 14.3 %copy-start.18 = (f32[3,3,1536]{2,0,1:T(4,128)S(1)}, f32[3,3,1536]{2,0,1:T(4,128)}, u32[]{:S(2)}) copy-start(f32[3,3,1536]{2,0,1:T(4,128)} %copy.285) | copy-start | bytes 165892
  303.8 14.3 %copy-start.19 = (f32[3,3,1536]{2,0,1:T(4,128)S(1)}, f32[3,3,1536]{2,0,1:T(4,128)}, u32[]{:S(2)}) copy-start(f32[3,3,1536]{2,0,1:T(4,128)} %copy.284) | copy-start | bytes 165892
  305.4 12.0 %copy-start.13 = (f32[1,1,8,4,1536]{4,2,3,1,0:T(8,128)}, f32[1,1,8,4,1536]{4,2,3,1,0:T(8,128)S(1)}, u32[]{:S(2)}) copy-start(f32[1,1,8,4,1536]{4,2,3,1,0:T(8,128)S(1)} %fusion.81) | copy-start | bytes 589828
  305.4 12.0 %collective-permute-start.3 = (f32[1,1,8,4,1536]{4,2,3,1,0:T(8,128)S(1)}, f32[1,1,8,4,1536]{4,2,3,1,0:T(8,128)S(1)}, u32[]{:S(2)}, u32[]{:S(2)}) collective-permute-start(f32[1,1,8,4,1536]{4,2,3,1,0:T(8,128)S(1)} %fusion.81), channel_id=1, source_target_pairs={{0,1},{1,2},{2,3},{3,4},{4,5},{5,6},{6,7},{8,9},{9,10},{10,11},{11... | collective-permute-start | bytes 589832 | tf_op jit(solution)/shard_map/ppermute | solution.py:29
  308.8 8.6 %collective-permute-start.2 = (f32[1,1,8,4,1536]{4,2,3,1,0:T(8,128)S(1)}, f32[1,1,8,4,1536]{4,2,3,1,0:T(8,128)S(1)}, u32[]{:S(2)}, u32[]{:S(2)}) collective-permute-start(f32[1,1,8,4,1536]{4,2,3,1,0:T(8,128)S(1)} %fusion.81), channel_id=1, source_target_pairs={{1,0},{2,1},{3,2},{4,3},{5,4},{6,5},{7,6},{9,8},{10,9},{11,10},{12... | collective-permute-start | bytes 589832 | tf_op jit(solution)/shard_map/ppermute | solution.py:30
  317.4 0.7 copy-start.14
  317.4 0.7 copy-start.15
  327.2 2.1 copy-start.7
  327.2 2.0 copy-start.34
  328.1 1.2 copy-start.6
  342.3 203.0 %reduce-scatter.5.cloned.1.call-start = ((), (), s32[]{:S(2)}) async-start(), calls=%async_computation.2 | async-start | bytes 2654208 | tf_op jit(solution)/shard_map/reduce_scatter | solution.py:270
  342.4 2.0 copy-start.12
  346.7 241.7 %all-reduce.10.cloned.1.call-start = ((), (), s32[]{:S(2)}) async-start(), calls=%async_computation.5 | async-start | bytes 2949120 | tf_op jit(solution)/shard_map/psum | solution.py:272
  362.0 4.3 copy-start.5
  362.0 4.3 copy-start.8
  362.0 4.3 copy-start.9
  362.0 4.3 copy-start.10
  368.3 6.6 %copy-start.30 = (f32[2,64]{1,0:T(2,128)S(1)}, f32[2,64]{1,0:T(2,128)}, u32[]{:S(2)}) copy-start(f32[2,64]{1,0:T(2,128)} %reduce_sum.86) | copy-start | bytes 1540
Sparse Core Ops, SparseCore 0:
  197.0 88.0 all-reduce.7
  342.4 130.7 reduce-scatter.6
  477.1 68.1 reduce-scatter.4
  547.9 40.4 all-reduce.9
where the time goes:
time: 606 us; the launch traced here: 601 us
  waiting for transfers between devices  235 us (39%)
  local copies, waits for them, and re-layouts  135 us (22%)
  matrix products  81.4 us (13%)
  blocking collectives  78.1 us (13%)
  other arithmetic  44.2 us (7%)
  between operations  14.8 us (2%)
  starting transfers between devices  12.8 us (2%)
    unnamed x6, waiting for transfers between devices  122 us
    reduce_scatter x1, waiting for transfers between devices, shards(): lax.psum_scatter(out_local, 'tm', scatter_dimension=0, tiled=True)  69.6 us
    psum x1, blocking collectives, shards(): lax.psum((kernel_local, gain_local), ('dp', 'tm'))  45 us
    psum x1, waiting for transfers between devices, shards(): shard_qkv, shard_out = lax.psum((partial_qkv, partial_out), 'dp')  37.9 us
    all_gather x1, blocking collectives, shards(): gathered = lax.all_gather(pooled, 'tm', axis=1, tiled=True)  33.1 us
    unnamed x75, local copies, waits for them, and re-layouts  21.8 us
  transfers between devices with their start and end apart: 8, of which 5 were waited for; matrix products, arithmetic and copies ran while one was open for 12% of the time, Pallas kernels for 0%

commit v1 on v0

v1 whole, which is shorter than its diff:
```python
import functools

import jax
import jax.numpy as jnp
import numpy as np
from jax import lax
from jax.experimental import pallas as pl
from jax.experimental.pallas import tpu as pltpu
from jax.sharding import PartitionSpec as P

HEADS = 12
GRID_H = 32
EPSILON = 1e-05
STRIDE = 4
LANES = 128
f32 = jnp.float32
bf16 = jnp.bfloat16
MESH = pl.DeviceIdType.MESH


def mm(a, b, ca=1, cb=0, precision=None):
    return lax.dot_general(
        a, b, (((ca,), (cb,)), ((), ())), preferred_element_type=f32, precision=precision
    )


def selection(cells, breadth):
    height = cells // breadth
    ph, pw = height // STRIDE, breadth // STRIDE
    sel = np.zeros((3, 3, ph, pw, height, breadth), np.float32)
    for b in range(3):
        for e in range(3):
            for i in range(ph):
                for u in range(pw):
                    y, x = STRIDE * i + b - 1, STRIDE * u + e - 1
                    if 0 <= y < height and 0 <= x < breadth:
                        sel[b, e, i, u, y, x] = 1.0
    return sel.reshape(9 * ph * pw, cells)


def stage_list(dp_size, tm_size):
    stages = []
    bit = 1
    while bit < dp_size:
        stages.append(("dp", bit))
        bit *= 2
    if tm_size > 1:
        stages.append(("tm", 1))
    bit = tm_size // 2
    while bit > 1:
        stages.append(("tm", bit))
        bit //= 2
    return stages


def block_index(stages, dp, tm):
    index = 0
    for axis, bit in stages:
        index = index * 2 + ((dp if axis == "dp" else tm) // bit) % 2
    return index


def kernel(
    dp_size, tm_size, stages, norm_scale,
    tok, wqkv, taps, wout, cot, sel,
    block_out, grad_tok, grad_qkv, grad_out, small_out,
    proj, blocks, dmix, mixed, dproj, gath, dpart, drecv,
    part_lo, part_mid, part_hi, in_lo, in_hi, normed, inv, dsum, in_next, in_prev,
    contrib, tok_t, acc, send, recv, fin, kacc, sbuf, srecv,
    halo_send, halo_recv, ag_send, ag_recv, rs_send, rs_recv,
    gr_send, gr_recv, sm_send, sm_recv, fin_send, fin_recv,
):
    cells, width = tok.shape
    wide = 2 * width
    pooled = sel.shape[0] // 9
    keys = tm_size * pooled
    scale = (width // HEADS) ** (-0.5)
    chunks = wide // LANES
    half_chunks = width // LANES
    rows = width // tm_size
    group = wide // dp_size
    blocks_all = dp_size * tm_size
    me_d = lax.axis_index("dp")
    me_t = lax.axis_index("tm")
    tile = 2 * LANES

    barrier = pltpu.get_barrier_semaphore()
    for k in range(1, tm_size):
        pl.semaphore_signal(
            barrier, inc=1, device_id={"tm": (me_t + k) % tm_size}, device_id_type=MESH
        )
    for k in range(1, dp_size):
        pl.semaphore_signal(
            barrier, inc=1, device_id={"dp": (me_d + k) % dp_size}, device_id_type=MESH
        )

    has_next = me_t < tm_size - 1
    has_prev = me_t > 0

    def remote(src, dst, ssem, rsem, where):
        return pltpu.make_async_remote_copy(
            src_ref=src, dst_ref=dst, send_sem=ssem, recv_sem=rsem,
            device_id=where, device_id_type=MESH,
        )

    def halo_up(src, dst, slot):
        return remote(src, dst, halo_send.at[slot], halo_recv.at[slot],
                      {"tm": (me_t + 1) % tm_size})

    def halo_down(src, dst, slot):
        return remote(src, dst, halo_send.at[slot], halo_recv.at[slot],
                      {"tm": (me_t + tm_size - 1) % tm_size})

    def halo_start(up_src, up_dst, down_src, down_dst, slot):
        @pl.when(has_next)
        def _():
            halo_up(up_src, up_dst, slot).start()

        @pl.when(has_prev)
        def _():
            halo_down(down_src, down_dst, slot + 1).start()

    def halo_wait(up_src, up_dst, down_src, down_dst, slot):
        @pl.when(has_next)
        def _():
            halo_up(up_src, up_dst, slot).wait_send()
            halo_down(down_src, down_dst, slot + 1).wait_recv()

        @pl.when(has_prev)
        def _():
            halo_down(down_src, down_dst, slot + 1).wait_send()
            halo_up(up_src, up_dst, slot).wait_recv()

    def cols(c, size=LANES, base=0):
        return pl.ds(pl.multiple_of(base + c * size, LANES), size)

    @pl.loop(0, wide // tile)
    def _(c):
        value = mm(tok[...], wqkv[:, cols(c, tile, width)]).astype(bf16)
        blocks[:, cols(c, tile)] = mm(sel[...], value).astype(bf16)

    @pl.loop(0, chunks)
    def _(c):
        s = c // half_chunks
        sums = [None, None, None]
        for p in range(9):
            value = blocks[p * pooled:(p + 1) * pooled, cols(c)].astype(f32)
            for t in range(3):
                term = value * taps[s, pl.ds(t * 9 + p, 1), :]
                sums[t] = term if sums[t] is None else sums[t] + term
        part_lo[:, cols(c)] = sums[0]
        part_mid[:, cols(c)] = sums[1]
        part_hi[:, cols(c)] = sums[2]

    pl.semaphore_wait(barrier, tm_size - 1 + dp_size - 1)
    first = (part_lo, in_lo, part_hi, in_hi, 0)
    halo_start(*first)

    @pl.when(jnp.logical_not(has_prev))
    def _():
        in_lo[...] = jnp.zeros_like(in_lo)

    @pl.when(jnp.logical_not(has_next))
    def _():
        in_hi[...] = jnp.zeros_like(in_hi)

    @pl.loop(0, width // tile)
    def _(c):
        proj[:, cols(c, tile)] = mm(tok[...], wqkv[:, cols(c, tile)]).astype(bf16)

    row = lax.broadcasted_iota(jnp.int32, (LANES, LANES), 0)
    col = lax.broadcasted_iota(jnp.int32, (LANES, LANES), 1)
    head = width // HEADS
    same = jnp.where((row < head) == (col < head), 1.0, 0.0).astype(f32)

    def group_mean(x):
        return mm(x, same, precision=lax.Precision.HIGHEST) * (1.0 / head)

    halo_wait(*first)

    @pl.loop(0, chunks)
    def _(c):
        s = c // half_chunks
        total = in_lo[:, cols(c)] + part_mid[:, cols(c)] + in_hi[:, cols(c)]
        centred = total - group_mean(total)
        inv_std = lax.rsqrt(group_mean(centred * centred) + EPSILON)
        norm = centred * inv_std
        normed[:, cols(c)] = norm
        inv[:, cols(c)] = inv_std
        gath[me_t, :, cols(c)] = (norm * taps[s, pl.ds(27, 1), :]).astype(bf16)

    def gather_copy(k):
        return remote(gath.at[me_t], gath.at[me_t], ag_send.at[k - 1], ag_recv.at[k - 1],
                      {"tm": (me_t + k) % tm_size})

    def gather_arrival(k):
        source = (me_t + tm_size - k) % tm_size
        return remote(gath.at[source], gath.at[source], ag_send.at[k - 1], ag_recv.at[k - 1],
                      {"tm": (me_t + k) % tm_size})

    for k in range(1, tm_size):
        gather_copy(k).start()

    @pl.loop(0, width // tile)
    def _(c):
        dmix[:, cols(c, tile)] = mm(
            cot[...], wout[pl.ds(pl.multiple_of(c * tile, tile), tile), :], 1, 1
        ).astype(bf16)

    @pl.loop(0, width // LANES)
    def _(c):
        tok_t[pl.ds(pl.multiple_of(c * LANES, LANES), LANES), :] = tok[:, cols(c)].T

    for k in range(1, tm_size):
        gather_copy(k).wait_send()
        gather_arrival(k).wait_recv()

    lane = lax.broadcasted_iota(jnp.int32, (1, LANES), 1)

    @pl.loop(0, half_chunks)
    def _(c):
        q = proj[:, cols(c)]
        k = gath[:, :, cols(c)].reshape(keys, LANES)
        v = gath[:, :, cols(c, LANES, width)].reshape(keys, LANES)
        dm = dmix[:, cols(c)]
        mixed_sum = q.astype(f32)
        dq_sum = dk_sum = dv_sum = None
        for a in range(2):
            mask = jnp.where((lane < head) == (a == 0), 1.0, 0.0).astype(f32)
            mask_b = mask.astype(bf16)
            k_a = k * mask_b
            scores = mm(q, k_a, 1, 1) * scale
            weights = jnp.exp(scores - jnp.max(scores, axis=-1, keepdims=True))
            inv_total = 1.0 / jnp.sum(weights, axis=-1, keepdims=True)
            rounded = weights.astype(bf16)
            attended = mm(rounded, v) * inv_total * mask
            mixed_sum = mixed_sum + attended
            dm_a = dm * mask_b
            dm_f = dm_a.astype(f32)
            scaled_grad = (dm_f * inv_total).astype(bf16)
            dv = mm(rounded, scaled_grad, 0, 0)
            d_probs = mm(dm_a, v, 1, 1)
            delta = jnp.sum(dm_f * attended, axis=-1, keepdims=True)
            ds = (weights * inv_total * (d_probs - delta)).astype(bf16)
            dq = mm(ds, k_a)
            dk = mm(ds, q * mask_b, 0, 0)
            dq_sum = dq if a == 0 else dq_sum + dq
            dk_sum = dk if a == 0 else dk_sum + dk
            dv_sum = dv if a == 0 else dv_sum + dv
        mixed[:, cols(c)] = mixed_sum.astype(bf16)
        dproj[:, cols(c)] = (dq_sum * scale + dm.astype(f32)).astype(bf16)
        dpart[:, :, cols(c)] = (dk_sum * scale).astype(bf16).reshape(tm_size, pooled, LANES)
        dpart[:, :, cols(c, LANES, width)] = dv_sum.astype(bf16).reshape(tm_size, pooled, LANES)

    def scatter_copy(k):
        target = (me_t + k) % tm_size
        return remote(dpart.at[target], drecv.at[k - 1], rs_send.at[k - 1], rs_recv.at[k - 1],
                      {"tm": target})

    for k in range(1, tm_size):
        scatter_copy(k).start()

    starts = []
    at = 0
    for s in range(len(stages)):
        starts.append(at)
        at += blocks_all >> (s + 1)

    def my_bit(s):
        axis, bit = stages[s]
        return ((me_d if axis == "dp" else me_t) // bit) % 2

    def peer(s):
        axis, bit = stages[s]
        me = me_d if axis == "dp" else me_t
        return {axis: me + bit * (1 - 2 * my_bit(s))}

    def base(s):
        at = 0
        for i in range(s):
            at = at + my_bit(i) * (blocks_all >> (i + 1))
        return at

    def halving_copy(part, s):
        span = pl.ds(starts[s], blocks_all >> (s + 1))
        return remote(send.at[part, span], recv.at[part, span], gr_send.at[part, s],
                      gr_recv.at[part, s], peer(s))

    def halving_start(part, s):
        count = blocks_all >> (s + 1)
        other = base(s) + (1 - my_bit(s)) * count

        @pl.loop(0, count)
        def _(i):
            send[part, starts[s] + i] = acc[part, other + i].astype(bf16)

        halving_copy(part, s).start()

    def halving_wait(part, s):
        count = blocks_all >> (s + 1)
        mine = base(s) + my_bit(s) * count
        halving_copy(part, s).wait()

        @pl.loop(0, count)
        def _(i):
            acc[part, mine + i] = acc[part, mine + i] + recv[part, starts[s] + i].astype(f32)

    def put(part, column, value):
        size = value.shape[1]
        value = value.reshape(tm_size, rows, size)
        for w in range(0, size, LANES):
            g, inside = divmod(column + w, group)
            for j in range(tm_size):
                acc[part, block_index(stages, g, j), :, inside:inside + LANES] = (
                    value[j, :, w:w + LANES]
                )

    def fin_copy(part, k):
        return remote(fin.at[part, 0], fin.at[part, k], fin_send.at[part, k - 1],
                      fin_recv.at[part, k - 1], {"dp": (me_d + k) % dp_size})

    def fin_start(part):
        fin[part, 0] = (acc[part, base(len(stages))] * norm_scale).astype(bf16)
        for k in range(1, dp_size):
            fin_copy(part, k).start()

    def fin_wait(part):
        for k in range(1, dp_size):
            fin_copy(part, k).wait()

    for c in range(width // tile):
        put(0, c * tile, mm(mixed[...], cot[:, c * tile:(c + 1) * tile], 0, 0))
    for c in range(width // tile):
        put(0, width + c * tile, mm(tok_t[...], dproj[:, c * tile:(c + 1) * tile]))
    halving_start(0, 0)

    @pl.loop(0, width // tile)
    def _(c):
        block_out[:, cols(c, tile)] = mm(mixed[...], wout[:, cols(c, tile)]).astype(bf16)

    halving_wait(0, 0)
    halving_start(0, 1)

    for k in range(1, tm_size):
        scatter_copy(k).wait()

    kacc[...] = jnp.zeros_like(kacc)

    def fold(x):
        return jnp.sum(x.reshape(pooled // 8, 8, LANES), axis=0)

    @pl.loop(0, chunks)
    def _(c):
        s = c // half_chunks
        total = dpart[me_t, :, cols(c)].astype(f32)
        for k in range(1, tm_size):
            total = total + drecv[k - 1, :, cols(c)].astype(f32)
        norm = normed[:, cols(c)]
        kacc[s, 27] += fold(total * norm)
        dn = total * taps[s, pl.ds(27, 1), :]
        dsum[:, cols(c)] = inv[:, cols(c)] * (
            dn - group_mean(dn) - norm * group_mean(dn * norm)
        )

    second = (dsum, in_prev, dsum, in_next, 2)
    halo_start(*second)

    @pl.when(jnp.logical_not(has_prev))
    def _():
        in_prev[...] = jnp.zeros_like(in_prev)

    @pl.when(jnp.logical_not(has_next))
    def _():
        in_next[...] = jnp.zeros_like(in_next)

    halving_wait(0, 1)
    halo_wait(*second)
    halving_start(0, 2)

    @pl.loop(0, chunks)
    def _(c):
        s = c // half_chunks
        shifted = (in_next[:, cols(c)], dsum[:, cols(c)], in_prev[:, cols(c)])
        for p in range(9):
            value = blocks[p * pooled:(p + 1) * pooled, cols(c)].astype(f32)
            spread = None
            for t in range(3):
                kacc[s, t * 9 + p] += fold(shifted[t] * value)
                term = shifted[t] * taps[s, pl.ds(t * 9 + p, 1), :]
                spread = term if spread is None else spread + term
            contrib[p * pooled:(p + 1) * pooled, cols(c)] = spread.astype(bf16)

    sbuf[0] = jnp.sum(kacc[...], axis=2)

    for c in range(wide // tile):
        dv = mm(sel[...], contrib[:, c * tile:(c + 1) * tile], 0, 0).astype(bf16)
        dproj[:, width + c * tile:width + (c + 1) * tile] = dv
        put(1, c * tile, mm(tok_t[...], dv))

    def small_copy(s):
        return remote(sbuf.at[s], srecv.at[s], sm_send.at[s], sm_recv.at[s], peer(s))

    def small_wait(s):
        small_copy(s).wait()
        sbuf[s + 1] = sbuf[s] + srecv[s]

    count = len(stages)
    halving_start(1, 0)
    small_copy(0).start()

    @pl.loop(0, width // tile)
    def _(c):
        at = pl.ds(pl.multiple_of(c * tile, tile), tile)
        grad_tok[:, cols(c, tile)] = mm(dproj[...], wqkv[at, :], 1, 1).astype(bf16)

    halving_wait(1, 0)
    small_wait(0)
    later = 3
    done = False
    for s in range(1, count):
        halving_start(1, s)
        small_copy(s).start()
        if later <= count:
            halving_wait(0, later - 1)
            if later < count:
                halving_start(0, later)
            later += 1
        elif not done:
            fin_start(0)
            done = True
        halving_wait(1, s)
        small_wait(s)
    while later <= count:
        halving_wait(0, later - 1)
        if later < count:
            halving_start(0, later)
        later += 1
    if not done:
        fin_start(0)
    fin_start(1)
    small_out[...] = sbuf[count] * norm_scale
    fin_wait(0)
    fin_wait(1)
    for part in range(2):
        for k in range(dp_size):
            g = (me_d + dp_size - k) % dp_size
            for w in range(0, group, LANES):
                value = fin[part, k, :, w:w + LANES].astype(f32)
                if part == 1:
                    grad_qkv[:, cols(0, LANES, width + g * group + w)] = value
                else:
                    column = g * group + w

                    @pl.when(column < width)
                    def _(value=value, column=column):
                        grad_out[:, cols(0, LANES, column % width)] = value

                    @pl.when(column >= width)
                    def _(value=value, column=column):
                        grad_qkv[:, cols(0, LANES, column % width)] = value


def shards(dp_size, tm_size, tokens, qkv_weight, pool_kernel, norm_gain, out_weight, cotangent):
    cells, width = tokens.shape[2:]
    wide = 2 * width
    stages = stage_list(dp_size, tm_size)
    blocks_all = dp_size * tm_size
    sel = jnp.asarray(selection(cells, cells // GRID_H), bf16)
    pooled = sel.shape[0] // 9
    rows = width // tm_size
    group = wide // dp_size
    norm_scale = float(blocks_all * cells) ** (-0.5)
    taps = jnp.concatenate([pool_kernel, norm_gain[:, None, :]], axis=1)
    taps = jnp.concatenate([taps, taps], axis=-1)
    taps_rows = taps.shape[1]
    vmem = pl.BlockSpec(memory_space=pltpu.VMEM)
    count = len(stages)
    dma = pltpu.SemaphoreType.DMA
    small = (pooled, wide)
    block_out, grad_tok, grad_qkv, grad_out, total = pl.pallas_call(
        functools.partial(kernel, dp_size, tm_size, stages, norm_scale),
        out_shape=[
            jax.ShapeDtypeStruct((cells, width), bf16),
            jax.ShapeDtypeStruct((cells, width), bf16),
            jax.ShapeDtypeStruct((rows, 3 * width), f32),
            jax.ShapeDtypeStruct((rows, width), f32),
            jax.ShapeDtypeStruct((2, taps_rows, LANES), f32),
        ],
        in_specs=[vmem] * 6,
        out_specs=[vmem] * 5,
        scratch_shapes=[
            pltpu.VMEM((cells, width), bf16),
            pltpu.VMEM((9 * pooled, wide), bf16),
            pltpu.VMEM((cells, width), bf16),
            pltpu.VMEM((cells, width), bf16),
            pltpu.VMEM((cells, 3 * width), bf16),
            pltpu.VMEM((tm_size, pooled, wide), bf16),
            pltpu.VMEM((tm_size, pooled, wide), bf16),
            pltpu.VMEM((tm_size - 1, pooled, wide), bf16),
        ]
        + [pltpu.VMEM(small, f32)] * 10
        + [
            pltpu.VMEM((9 * pooled, wide), bf16),
            pltpu.VMEM((width, cells), bf16),
            pltpu.VMEM((2, blocks_all, rows, group), f32),
            pltpu.VMEM((2, blocks_all, rows, group), bf16),
            pltpu.VMEM((2, blocks_all, rows, group), bf16),
            pltpu.VMEM((2, dp_size, rows, group), bf16),
            pltpu.VMEM((2, taps_rows, 8, LANES), f32),
            pltpu.VMEM((count + 1, 2, taps_rows, LANES), f32),
            pltpu.VMEM((count, 2, taps_rows, LANES), f32),
            dma((4,)),
            dma((4,)),
            dma((tm_size - 1,)),
            dma((tm_size - 1,)),
            dma((tm_size - 1,)),
            dma((tm_size - 1,)),
            dma((2, count)),
            dma((2, count)),
            dma((count,)),
            dma((count,)),
            dma((2, dp_size - 1)),
            dma((2, dp_size - 1)),
        ],
        compiler_params=pltpu.CompilerParams(
            collective_id=0, has_side_effects=True, vmem_limit_bytes=63 * 1024 * 1024
        ),
        cost_estimate=pl.CostEstimate(
            flops=10 * 10**9, bytes_accessed=10 * 10**6, transcendentals=0
        ),
    )(
        tokens.reshape(cells, width), qkv_weight, taps, out_weight,
        cotangent.reshape(cells, width), sel,
    )
    head = width // HEADS
    summed = total[:, :, :head] + total[:, :, head:]
    return (
        block_out.reshape(tokens.shape), grad_tok.reshape(tokens.shape), grad_qkv, grad_out,
        summed[:, :-1], summed[:, -1],
    )


def solution(mesh):
    placed = (P("dp", "tm", None, None), P(), P(), P(), P(), P("dp", "tm", None, None))
    return jax.shard_map(
        functools.partial(shards, mesh.shape["dp"], mesh.shape["tm"]),
        mesh=mesh,
        in_specs=placed,
        out_specs=(
            P("dp", "tm", None, None),
            P("dp", "tm", None, None),
            P("tm", None),
            P("tm", None),
            P(),
            P(),
        ),
        check_vma=False,
    )
```

time: 606 us -> 143 us (0.24)
  waiting for transfers between devices: 235 us -> 0 us
  Pallas kernels: 0 us -> 131 us
  local copies, waits for them, and re-layouts: 135 us -> 7.71 us
  matrix products: 81.4 us -> 0 us
  blocking collectives: 78.1 us -> 0 us
  other arithmetic: 44.2 us -> 2.39 us
  between operations: 14.8 us -> 0.66 us
  starting transfers between devices: 12.8 us -> 0 us
    pallas_call x0 -> x1, Pallas kernels: none -> 131 us  [shards(): pl.pallas_call(functools.partial(kernel, dp_size, tm_size, stages, norm_s...]
    unnamed x6 -> x0, waiting for transfers between devices: 122 us -> none
    dot_general x48 -> x0, matrix products: 81.4 us -> none  [the longest x6 11.1 us: group_backward(): jnp.einsum('crgk,crgd->ckgd', d_scores, queries, preferred_element_type=j...]
    reduce_scatter x1 -> x0, waiting for transfers between devices: 69.6 us -> none  [shards(): lax.psum_scatter(out_local, 'tm', scatter_dimension=0, tiled=True)]
    psum x1 -> x0, blocking collectives: 45 us -> none  [shards(): lax.psum((kernel_local, gain_local), ('dp', 'tm'))]
    psum x1 -> x0, waiting for transfers between devices: 37.9 us -> none  [shards(): shard_qkv, shard_out = lax.psum((partial_qkv, partial_out), 'dp')]
    all_gather x1 -> x0, blocking collectives: 33.1 us -> none  [shards(): gathered = lax.all_gather(pooled, 'tm', axis=1, tiled=True)]
    reshape x11 -> x0, local copies, waits for them, and re-layouts: 24.7 us -> none  [the longest x1 4.24 us: cut_blocks(): padded.reshape(extent[:-3] + (pooled_h + 1, 4, pooled_w + 1, 4, extent[-1]))]
  transfers between devices with their start and end apart: 8 -> 0, of which waited for: 5 -> 0; matrix products, arithmetic and copies ran while one was open for 12% -> 0% of each run, Pallas kernels for 0% -> 0%
where the time goes in v1:
time: 143 us; the launch traced here: 142 us
  Pallas kernels  131 us (92%)
  local copies, waits for them, and re-layouts  7.71 us (5%)
  other arithmetic  2.39 us (2%)
    pallas_call x1, Pallas kernels, shards(): pl.pallas_call(functools.partial(kernel, dp_size, tm_size, stages, norm_s...  131 us
    unnamed x10, local copies, waits for them, and re-layouts  7.14 us

profile of v1, /device:TPU:0, one launch (start us, length us, event | category | flops | bytes accessed | tf_op | source)
XLA Modules:
  0.0 142.2 jit_solution(5054543073461044416)
XLA Ops:
  0.6 0.7 copy.13
  1.4 1.4 %maximum_maximum_fusion.taps = f32[2,28,128]{2,1,0:T(8,128)} fusion(f32[2,1,64]{2,1,0:T(1,128)} %bitcast.12, f32[2,27,64]{2,1,0:T(8,128)S(1)} %copy.13), kind=kLoop, calls=%fused_computation | loop fusion | flops 21504 | bytes 43008 | tf_op jit(solution)/shard_map/concatenate | solution.py:474
  2.8 131.5 %shard_map.118 = (bf16[512,768]{1,0:T(8,128)(2,1)}, bf16[512,768]{1,0:T(8,128)(2,1)}, f32[96,2304]{1,0:T(8,128)}, f32[96,768]{1,0:T(8,128)}, f32[2,28,128]{2,1,0:T(8,128)}) custom-call(bf16[512,768]{1,0:T(8,128)(2,1)} %bitcast.14, bf16[768,2304]{1,0:T(8,128)(2,1)} %wqkv.1, f32[2,28,128]{2,1,0:T(8,128)} %maximum_maximum_fusion.taps, bf16[768,768]{1,0:T(8,128)(2,1)} %wout.1, ...), custom_call_target="tpu_custom_call" | custom-call | flops 10000000000 | bytes 10000000 | tf_op jit(solution)/shard_map/pallas_call | solution.py:480
  134.3 0.0 copy-start
  134.3 0.0 copy-start.1
  134.3 0.9 slice_add_fusion
  135.3 0.6 slice.17
  135.8 0.6 copy.15
  136.5 2.1 %copy.20 = bf16[1,1,512,768]{3,2,1,0:T(8,128)(2,1)} copy(bf16[1,1,512,768]{3,2,1,0:T(8,128)(2,1)} %bitcast.10) | data formatting | bytes 1572864
  138.5 2.1 %copy.21 = bf16[1,1,512,768]{3,2,1,0:T(8,128)(2,1)} copy(bf16[1,1,512,768]{3,2,1,0:T(8,128)(2,1)} %bitcast.9) | data formatting | bytes 1572864
  140.6 0.0 copy-done
  140.6 0.9 copy.22
  141.5 0.0 copy-done.1
  141.5 0.7 copy.23
Async XLA Ops:
  134.3 6.3 %copy-start = (f32[96,2304]{1,0:T(8,128)S(1)}, f32[96,2304]{1,0:T(8,128)}, u32[]{:S(2)}) copy-start(f32[96,2304]{1,0:T(8,128)} %get-tuple-element.30) | copy-start | bytes 2654212
  134.3 7.2 %copy-start.1 = (f32[96,768]{1,0:T(8,128)S(1)}, f32[96,768]{1,0:T(8,128)}, u32[]{:S(2)}) copy-start(f32[96,768]{1,0:T(8,128)} %get-tuple-element.31) | copy-start | bytes 884740

commit v2 on v1

v2 whole, which is shorter than its diff:
```python
import functools

import jax
import jax.numpy as jnp
import numpy as np
from jax import lax
from jax.experimental import pallas as pl
from jax.experimental.pallas import tpu as pltpu
from jax.sharding import PartitionSpec as P

HEADS = 12
GRID_H = 32
EPSILON = 1e-05
STRIDE = 4
LANES = 128
f32 = jnp.float32
bf16 = jnp.bfloat16
MESH = pl.DeviceIdType.MESH


def mm(a, b, ca=1, cb=0, precision=None):
    return lax.dot_general(
        a, b, (((ca,), (cb,)), ((), ())), preferred_element_type=f32, precision=precision
    )


def selection(cells, breadth):
    height = cells // breadth
    ph, pw = height // STRIDE, breadth // STRIDE
    sel = np.zeros((3, 3, ph, pw, height, breadth), np.float32)
    for b in range(3):
        for e in range(3):
            for i in range(ph):
                for u in range(pw):
                    y, x = STRIDE * i + b - 1, STRIDE * u + e - 1
                    if 0 <= y < height and 0 <= x < breadth:
                        sel[b, e, i, u, y, x] = 1.0
    return sel.reshape(9 * ph * pw, cells)


def stage_list(dp_size, tm_size, dp_first):
    over_dp, over_tm = [], []
    bit = 1
    while bit < dp_size:
        over_dp.append(("dp", bit))
        bit *= 2
    if tm_size > 1:
        over_tm.append(("tm", 1))
    bit = tm_size // 2
    while bit > 1:
        over_tm.append(("tm", bit))
        bit //= 2
    if dp_first:
        return over_dp + over_tm
    return over_dp[:1] + over_tm + over_dp[1:]


def block_index(stages, dp, tm):
    index = 0
    for axis, bit in stages:
        index = index * 2 + ((dp if axis == "dp" else tm) // bit) % 2
    return index


def kernel(
    dp_size, tm_size, orders, norm_scale,
    tok, wqkv, taps, wout, cot, sel,
    block_out, grad_tok, grad_qkv, grad_out, small_out,
    proj, blocks, dmix, mixed, dproj, gath, dpart, drecv,
    zsend, zrecv, part_lo, part_mid, part_hi, in_lo, in_hi, normed, inv, dsum,
    dsum_b, in_next, in_prev, contrib, tok_t,
    acc_a, acc_b, acc_c, send_a, send_b, send_c, recv_a, recv_b, recv_c, fin_a, fin_b, fin_c,
    kacc, sbuf, srecv,
    halo_send, halo_recv, ag_send, ag_recv, rs_send, rs_recv, rz_send, rz_recv,
    gr_send, gr_recv, sm_send, sm_recv, fin_send, fin_recv,
):
    cells, width = tok.shape
    wide = 2 * width
    pooled = sel.shape[0] // 9
    keys = tm_size * pooled
    scale = (width // HEADS) ** (-0.5)
    chunks = wide // LANES
    half_chunks = width // LANES
    rows = width // tm_size
    group = wide // dp_size
    blocks_all = dp_size * tm_size
    me_d = lax.axis_index("dp")
    me_t = lax.axis_index("tm")
    tile = 2 * LANES
    column = tm_size // 2
    pair = me_t + 1 - 2 * (me_t % 2)
    third = half_chunks // 2
    accs, sends, recvs = (acc_a, acc_b, acc_c), (send_a, send_b, send_c), (recv_a, recv_b, recv_c)
    fins = (fin_a, fin_b, fin_c)

    barrier = pltpu.get_barrier_semaphore()
    for k in range(1, tm_size):
        pl.semaphore_signal(
            barrier, inc=1, device_id={"tm": (me_t + k) % tm_size}, device_id_type=MESH
        )
    for k in range(1, dp_size):
        pl.semaphore_signal(
            barrier, inc=1, device_id={"dp": (me_d + k) % dp_size}, device_id_type=MESH
        )

    has_next = me_t < tm_size - 1
    has_prev = me_t > 0

    def remote(src, dst, ssem, rsem, where):
        return pltpu.make_async_remote_copy(
            src_ref=src, dst_ref=dst, send_sem=ssem, recv_sem=rsem,
            device_id=where, device_id_type=MESH,
        )

    def halo_up(src, dst, slot):
        return remote(src, dst, halo_send.at[slot], halo_recv.at[slot],
                      {"tm": (me_t + 1) % tm_size})

    def halo_down(src, dst, slot):
        return remote(src, dst, halo_send.at[slot], halo_recv.at[slot],
                      {"tm": (me_t + tm_size - 1) % tm_size})

    def halo_start(up_src, up_dst, down_src, down_dst, slot):
        @pl.when(has_next)
        def _():
            halo_up(up_src, up_dst, slot).start()

        @pl.when(has_prev)
        def _():
            halo_down(down_src, down_dst, slot + 1).start()

    def halo_wait(up_src, up_dst, down_src, down_dst, slot):
        @pl.when(has_next)
        def _():
            halo_up(up_src, up_dst, slot).wait_send()
            halo_down(down_src, down_dst, slot + 1).wait_recv()

        @pl.when(has_prev)
        def _():
            halo_down(down_src, down_dst, slot + 1).wait_send()
            halo_up(up_src, up_dst, slot).wait_recv()

    def cols(c, size=LANES, base=0):
        return pl.ds(pl.multiple_of(base + c * size, LANES), size)

    def first(s):
        at = pl.ds(s * width, width)
        return (part_lo.at[:, at], in_lo.at[:, at], part_hi.at[:, at], in_hi.at[:, at], 2 * s)

    for s in range(2):
        @pl.loop(0, width // tile)
        def _(c, s=s):
            value = mm(tok[...], wqkv[:, cols(c, tile, width + s * width)]).astype(bf16)
            blocks[:, cols(c, tile, s * width)] = mm(sel[...], value).astype(bf16)

        @pl.loop(0, half_chunks)
        def _(c, s=s):
            here = cols(c, LANES, s * width)
            sums = [None, None, None]
            for p in range(9):
                value = blocks[p * pooled:(p + 1) * pooled, here].astype(f32)
                for t in range(3):
                    term = value * taps[s, pl.ds(t * 9 + p, 1), :]
                    sums[t] = term if sums[t] is None else sums[t] + term
            part_lo[:, here] = sums[0]
            part_mid[:, here] = sums[1]
            part_hi[:, here] = sums[2]

        if s == 0:
            pl.semaphore_wait(barrier, tm_size - 1 + dp_size - 1)
        halo_start(*first(s))

    @pl.when(jnp.logical_not(has_prev))
    def _():
        in_lo[...] = jnp.zeros_like(in_lo)

    @pl.when(jnp.logical_not(has_next))
    def _():
        in_hi[...] = jnp.zeros_like(in_hi)

    @pl.loop(0, width // tile)
    def _(c):
        proj[:, cols(c, tile)] = mm(tok[...], wqkv[:, cols(c, tile)]).astype(bf16)

    row = lax.broadcasted_iota(jnp.int32, (LANES, LANES), 0)
    col = lax.broadcasted_iota(jnp.int32, (LANES, LANES), 1)
    head = width // HEADS
    same = jnp.where((row < head) == (col < head), 1.0, 0.0).astype(f32)

    def group_mean(x):
        return mm(x, same, precision=lax.Precision.HIGHEST) * (1.0 / head)

    for s in range(2):
        halo_wait(*first(s))

    @pl.loop(0, chunks)
    def _(c):
        s = c // half_chunks
        total = in_lo[:, cols(c)] + part_mid[:, cols(c)] + in_hi[:, cols(c)]
        centred = total - group_mean(total)
        inv_std = lax.rsqrt(group_mean(centred * centred) + EPSILON)
        norm = centred * inv_std
        normed[:, cols(c)] = norm
        inv[:, cols(c)] = inv_std
        gath[me_t, :, cols(c)] = (norm * taps[s, pl.ds(27, 1), :]).astype(bf16)

    def column_slot(k, back):
        return (back + tm_size - 2 * k) % tm_size

    def along(k, slot):
        return remote(gath.at[slot], gath.at[slot], ag_send.at[0, k], ag_recv.at[0, k],
                      {"tm": (me_t + 2 * k) % tm_size})

    def across(k, slot):
        return remote(gath.at[slot], gath.at[slot], ag_send.at[1, k], ag_recv.at[1, k],
                      {"tm": pair})

    for k in range(1, column):
        along(k, me_t).start()
    across(0, me_t).start()

    @pl.loop(0, width // tile)
    def _(c):
        dmix[:, cols(c, tile)] = mm(
            cot[...], wout[pl.ds(pl.multiple_of(c * tile, tile), tile), :], 1, 1
        ).astype(bf16)

    for k in range(1, column):
        along(k, column_slot(k, me_t)).wait_recv()
        across(k, column_slot(k, me_t)).start()

    @pl.loop(0, width // LANES)
    def _(c):
        tok_t[pl.ds(pl.multiple_of(c * LANES, LANES), LANES), :] = tok[:, cols(c)].T

    for k in range(1, column):
        along(k, me_t).wait_send()
    for k in range(column):
        across(k, column_slot(k, pair)).wait_recv()
        across(k, column_slot(k, me_t)).wait_send()

    lane = lax.broadcasted_iota(jnp.int32, (1, LANES), 1)

    def attention(h, i):
        c = h * third + i
        q = proj[:, cols(c)]
        k = gath[:, :, cols(c)].reshape(keys, LANES)
        v = gath[:, :, cols(c, LANES, width)].reshape(keys, LANES)
        dm = dmix[:, cols(c)]
        mixed_sum = q.astype(f32)
        dq_sum = dk_sum = dv_sum = None
        for a in range(2):
            mask = jnp.where((lane < head) == (a == 0), 1.0, 0.0).astype(f32)
            mask_b = mask.astype(bf16)
            k_a = k * mask_b
            scores = mm(q, k_a, 1, 1) * scale
            weights = jnp.exp(scores - jnp.max(scores, axis=-1, keepdims=True))
            inv_total = 1.0 / jnp.sum(weights, axis=-1, keepdims=True)
            rounded = weights.astype(bf16)
            attended = mm(rounded, v) * inv_total * mask
            mixed_sum = mixed_sum + attended
            dm_a = dm * mask_b
            dm_f = dm_a.astype(f32)
            scaled_grad = (dm_f * inv_total).astype(bf16)
            dv = mm(rounded, scaled_grad, 0, 0)
            d_probs = mm(dm_a, v, 1, 1)
            delta = jnp.sum(dm_f * attended, axis=-1, keepdims=True)
            ds = (weights * inv_total * (d_probs - delta)).astype(bf16)
            dq = mm(ds, k_a)
            dk = mm(ds, q * mask_b, 0, 0)
            dq_sum = dq if a == 0 else dq_sum + dq
            dk_sum = dk if a == 0 else dk_sum + dk
            dv_sum = dv if a == 0 else dv_sum + dv
        mixed[:, cols(c)] = mixed_sum.astype(bf16)
        dproj[:, cols(c)] = (dq_sum * scale + dm.astype(f32)).astype(bf16)
        shape = (tm_size, pooled, LANES)
        dpart[h, :, :, cols(i)] = (dk_sum * scale).astype(bf16).reshape(shape)
        dpart[h, :, :, cols(third + i)] = dv_sum.astype(bf16).reshape(shape)

    def reduce_across(h, k):
        return remote(dpart.at[h, (pair + 2 * k) % tm_size], drecv.at[h, k], rs_send.at[h, k],
                      rs_recv.at[h, k], {"tm": pair})

    def reduce_along(h, k):
        return remote(zsend.at[h, k - 1], zrecv.at[h, k - 1], rz_send.at[h, k - 1],
                      rz_recv.at[h, k - 1], {"tm": (me_t + 2 * k) % tm_size})

    def pass_on(h):
        for k in range(1, column):
            reduce_across(h, k).wait()
            mine = dpart[h, (me_t + 2 * k) % tm_size].astype(f32)
            zsend[h, k - 1] = (mine + drecv[h, k].astype(f32)).astype(bf16)
            reduce_along(h, k).start()
        reduce_across(h, 0).wait()

    for h in range(2):
        @pl.loop(0, third)
        def _(i, h=h):
            attention(h, i)

        for k in list(range(1, column)) + [0]:
            reduce_across(h, k).start()

    count = len(orders[0])
    starts = []
    at = 0
    for s in range(count):
        starts.append(at)
        at += blocks_all >> (s + 1)

    def my_bit(part, s):
        axis, bit = orders[part][s]
        return ((me_d if axis == "dp" else me_t) // bit) % 2

    def peer(part, s):
        axis, bit = orders[part][s]
        me = me_d if axis == "dp" else me_t
        return {axis: me + bit * (1 - 2 * my_bit(part, s))}

    def base(part, s):
        at = 0
        for i in range(s):
            at = at + my_bit(part, i) * (blocks_all >> (i + 1))
        return at

    def halving_copy(part, s):
        span = pl.ds(starts[s], blocks_all >> (s + 1))
        return remote(sends[part].at[span], recvs[part].at[span], gr_send.at[part, s],
                      gr_recv.at[part, s], peer(part, s))

    def halving_start(part, s):
        size = blocks_all >> (s + 1)
        other = base(part, s) + (1 - my_bit(part, s)) * size

        @pl.loop(0, size)
        def _(i):
            sends[part][starts[s] + i] = accs[part][other + i].astype(bf16)

        halving_copy(part, s).start()

    def halving_wait(part, s):
        size = blocks_all >> (s + 1)
        mine = base(part, s) + my_bit(part, s) * size
        halving_copy(part, s).wait()

        @pl.loop(0, size)
        def _(i):
            accs[part][mine + i] += recvs[part][starts[s] + i].astype(f32)

    def put(part, g, inside, value):
        value = value.reshape(tm_size, rows, LANES)
        for j in range(tm_size):
            accs[part][block_index(orders[part], g, j), :, inside:inside + LANES] = value[j]

    per_group = group // LANES

    def put_first(at, value):
        for w in range(0, tile, LANES):
            g, r = divmod((at + w) // LANES, per_group)
            put(0, g, r * LANES, value[:, w:w + LANES])

    def put_second(at, value):
        for w in range(0, tile, LANES):
            g, r = divmod((at + w) // LANES, per_group)
            if r < per_group - 1:
                put(1, g, r * LANES, value[:, w:w + LANES])
            else:
                put(2, g, 0, value[:, w:w + LANES])

    def fin_copy(part, k):
        return remote(fins[part].at[0], fins[part].at[k], fin_send.at[part, k - 1],
                      fin_recv.at[part, k - 1], {"dp": (me_d + k) % dp_size})

    def fin_start(part):
        fins[part][0] = (accs[part][base(part, count)] * norm_scale).astype(bf16)
        for k in range(1, dp_size):
            fin_copy(part, k).start()

    def fin_wait(part):
        for k in range(1, dp_size):
            fin_copy(part, k).wait()

    def small_copy(s):
        return remote(sbuf.at[s], srecv.at[s], sm_send.at[s], sm_recv.at[s], peer(1, s))

    progress = [-1, -1, -1]

    def advance(part):
        s = progress[part]
        if s == count:
            return
        if s >= 0:
            halving_wait(part, s)
            if part == 1:
                small_copy(s).wait()
                sbuf[s + 1] = sbuf[s] + srecv[s]
        progress[part] = s + 1
        if s + 1 == count:
            fin_start(part)
            return
        halving_start(part, s + 1)
        if part == 1:
            small_copy(s + 1).start()

    pass_on(0)
    for c in range(width // tile):
        put_first(c * tile, mm(mixed[...], cot[:, c * tile:(c + 1) * tile], 0, 0))
    for c in range(width // tile):
        put_first(width + c * tile, mm(tok_t[...], dproj[:, c * tile:(c + 1) * tile]))
    advance(0)
    pass_on(1)

    @pl.loop(0, width // tile)
    def _(c):
        block_out[:, cols(c, tile)] = mm(mixed[...], wout[:, cols(c, tile)]).astype(bf16)

    advance(0)

    for h in range(2):
        for k in range(1, column):
            reduce_along(h, k).wait()

    kacc[...] = jnp.zeros_like(kacc)

    def fold(x):
        return jnp.sum(x.reshape(pooled // 8, 8, LANES), axis=0)

    @pl.loop(0, chunks)
    def _(c):
        s = c // half_chunks
        h = (c % half_chunks) // third
        here = cols(s * third + c % third)
        total = dpart[h, me_t, :, here].astype(f32) + drecv[h, 0, :, here].astype(f32)
        for k in range(1, column):
            total = total + zrecv[h, k - 1, :, here].astype(f32)
        norm = normed[:, cols(c)]
        kacc[s, 27] += fold(total * norm)
        dn = total * taps[s, pl.ds(27, 1), :]
        value = inv[:, cols(c)] * (dn - group_mean(dn) - norm * group_mean(dn * norm))
        dsum[:, cols(c)] = value
        dsum_b[:, cols(c)] = value.astype(bf16)

    second = (dsum_b, in_prev, dsum_b, in_next, 4)
    halo_start(*second)

    @pl.when(jnp.logical_not(has_prev))
    def _():
        in_prev[...] = jnp.zeros_like(in_prev)

    @pl.when(jnp.logical_not(has_next))
    def _():
        in_next[...] = jnp.zeros_like(in_next)

    halo_wait(*second)
    advance(0)

    @pl.loop(0, chunks)
    def _(c):
        s = c // half_chunks
        shifted = (
            in_next[:, cols(c)].astype(f32), dsum[:, cols(c)], in_prev[:, cols(c)].astype(f32)
        )
        for p in range(9):
            value = blocks[p * pooled:(p + 1) * pooled, cols(c)].astype(f32)
            spread = None
            for t in range(3):
                kacc[s, t * 9 + p] += fold(shifted[t] * value)
                term = shifted[t] * taps[s, pl.ds(t * 9 + p, 1), :]
                spread = term if spread is None else spread + term
            contrib[p * pooled:(p + 1) * pooled, cols(c)] = spread.astype(bf16)

    sbuf[0] = jnp.sum(kacc[...], axis=2)
    advance(0)

    for c in range(wide // tile):
        dv = mm(sel[...], contrib[:, c * tile:(c + 1) * tile], 0, 0).astype(bf16)
        dproj[:, width + c * tile:width + (c + 1) * tile] = dv
        put_second(c * tile, mm(tok_t[...], dv))

    advance(1)
    advance(2)
    advance(0)

    @pl.loop(0, width // tile)
    def _(c):
        at = pl.ds(pl.multiple_of(c * tile, tile), tile)
        grad_tok[:, cols(c, tile)] = mm(dproj[...], wqkv[at, :], 1, 1).astype(bf16)

    advance(2)
    advance(1)
    while min(progress) < count:
        advance(2)
        advance(1)
        advance(0)
    small_out[...] = sbuf[count] * norm_scale

    def write(at, value):
        if isinstance(at, tuple):
            grad_qkv[:, cols(0, LANES, at[0])] = value
            return

        @pl.when(at < width)
        def _():
            grad_out[:, cols(0, LANES, at % width)] = value

        @pl.when(at >= width)
        def _():
            grad_qkv[:, cols(0, LANES, at % width)] = value

    for part in (0, 2, 1):
        fin_wait(part)
        for k in range(dp_size):
            g = (me_d + dp_size - k) % dp_size
            for w in range(0, fins[part].shape[2], LANES):
                value = fins[part][k, :, w:w + LANES].astype(f32)
                at = g * group + w + (group - LANES if part == 2 else 0)
                write(at if part == 0 else (width + at,), value)


def shards(dp_size, tm_size, tokens, qkv_weight, pool_kernel, norm_gain, out_weight, cotangent):
    cells, width = tokens.shape[2:]
    wide = 2 * width
    orders = [stage_list(dp_size, tm_size, first) for first in (True, True, False)]
    blocks_all = dp_size * tm_size
    sel = jnp.asarray(selection(cells, cells // GRID_H), bf16)
    pooled = sel.shape[0] // 9
    rows = width // tm_size
    group = wide // dp_size
    norm_scale = float(blocks_all * cells) ** (-0.5)
    taps = jnp.concatenate([pool_kernel, norm_gain[:, None, :]], axis=1)
    taps = jnp.concatenate([taps, taps], axis=-1)
    taps_rows = taps.shape[1]
    vmem = pl.BlockSpec(memory_space=pltpu.VMEM)
    count = len(orders[0])
    column = tm_size // 2
    widths = (group, group - LANES, LANES)
    dma = pltpu.SemaphoreType.DMA
    small = (pooled, wide)
    block_out, grad_tok, grad_qkv, grad_out, total = pl.pallas_call(
        functools.partial(kernel, dp_size, tm_size, orders, norm_scale),
        out_shape=[
            jax.ShapeDtypeStruct((cells, width), bf16),
            jax.ShapeDtypeStruct((cells, width), bf16),
            jax.ShapeDtypeStruct((rows, 3 * width), f32),
            jax.ShapeDtypeStruct((rows, width), f32),
            jax.ShapeDtypeStruct((2, taps_rows, LANES), f32),
        ],
        in_specs=[vmem] * 6,
        out_specs=[vmem] * 5,
        scratch_shapes=[
            pltpu.VMEM((cells, width), bf16),
            pltpu.VMEM((9 * pooled, wide), bf16),
            pltpu.VMEM((cells, width), bf16),
            pltpu.VMEM((cells, width), bf16),
            pltpu.VMEM((cells, 3 * width), bf16),
            pltpu.VMEM((tm_size, pooled, wide), bf16),
            pltpu.VMEM((2, tm_size, pooled, width), bf16),
            pltpu.VMEM((2, column, pooled, width), bf16),
            pltpu.VMEM((2, column - 1, pooled, width), bf16),
            pltpu.VMEM((2, column - 1, pooled, width), bf16),
        ]
        + [pltpu.VMEM(small, f32)] * 8
        + [pltpu.VMEM(small, bf16)] * 3
        + [
            pltpu.VMEM((9 * pooled, wide), bf16),
            pltpu.VMEM((width, cells), bf16),
        ]
        + [pltpu.VMEM((blocks_all, rows, w), f32) for w in widths]
        + [pltpu.VMEM((blocks_all, rows, w), bf16) for w in widths * 2]
        + [pltpu.VMEM((dp_size, rows, w), bf16) for w in widths]
        + [
            pltpu.VMEM((2, taps_rows, 8, LANES), f32),
            pltpu.VMEM((count + 1, 2, taps_rows, LANES), f32),
            pltpu.VMEM((count, 2, taps_rows, LANES), f32),
            dma((6,)),
            dma((6,)),
            dma((2, column)),
            dma((2, column)),
            dma((2, column)),
            dma((2, column)),
            dma((2, column - 1)),
            dma((2, column - 1)),
            dma((3, count)),
            dma((3, count)),
            dma((count,)),
            dma((count,)),
            dma((3, dp_size - 1)),
            dma((3, dp_size - 1)),
        ],
        compiler_params=pltpu.CompilerParams(
            collective_id=0, has_side_effects=True, vmem_limit_bytes=63 * 1024 * 1024
        ),
        cost_estimate=pl.CostEstimate(
            flops=10 * 10**9, bytes_accessed=10 * 10**6, transcendentals=0
        ),
    )(
        tokens.reshape(cells, width), qkv_weight, taps, out_weight,
        cotangent.reshape(cells, width), sel,
    )
    head = width // HEADS
    summed = total[:, :, :head] + total[:, :, head:]
    return (
        block_out.reshape(tokens.shape), grad_tok.reshape(tokens.shape), grad_qkv, grad_out,
        summed[:, :-1], summed[:, -1],
    )


def solution(mesh):
    placed = (P("dp", "tm", None, None), P(), P(), P(), P(), P("dp", "tm", None, None))
    return jax.shard_map(
        functools.partial(shards, mesh.shape["dp"], mesh.shape["tm"]),
        mesh=mesh,
        in_specs=placed,
        out_specs=(
            P("dp", "tm", None, None),
            P("dp", "tm", None, None),
            P("tm", None),
            P("tm", None),
            P(),
            P(),
        ),
        check_vma=False,
    )
```

time: 143 us -> 126 us (0.88)
  Pallas kernels: 131 us -> 114 us
    pallas_call x1, Pallas kernels: 131 us -> 114 us  [shards(): pl.pallas_call(functools.partial(kernel, dp_size, tm_size, orders, norm_s...]
where the time goes in v2:
time: 126 us; the launch traced here: 125 us
  Pallas kernels  114 us (90%)
  local copies, waits for them, and re-layouts  7.71 us (6%)
  other arithmetic  2.39 us (2%)
    pallas_call x1, Pallas kernels, shards(): pl.pallas_call(functools.partial(kernel, dp_size, tm_size, orders, norm_s...  114 us
    unnamed x10, local copies, waits for them, and re-layouts  7.14 us

profile of v2, /device:TPU:0, one launch (start us, length us, event | category | flops | bytes accessed | tf_op | source)
XLA Modules:
  0.0 125.2 jit_solution(16108963196381917665)
XLA Ops:
  0.6 0.7 copy.13
  1.4 1.4 %maximum_maximum_fusion.taps = f32[2,28,128]{2,1,0:T(8,128)} fusion(f32[2,1,64]{2,1,0:T(1,128)} %bitcast.12, f32[2,27,64]{2,1,0:T(8,128)S(1)} %copy.13), kind=kLoop, calls=%fused_computation | loop fusion | flops 21504 | bytes 43008 | tf_op jit(solution)/shard_map/concatenate | solution.py:531
  2.8 114.5 %shard_map.118 = (bf16[512,768]{1,0:T(8,128)(2,1)}, bf16[512,768]{1,0:T(8,128)(2,1)}, f32[96,2304]{1,0:T(8,128)}, f32[96,768]{1,0:T(8,128)}, f32[2,28,128]{2,1,0:T(8,128)}) custom-call(bf16[512,768]{1,0:T(8,128)(2,1)} %bitcast.14, bf16[768,2304]{1,0:T(8,128)(2,1)} %wqkv.1, f32[2,28,128]{2,1,0:T(8,128)} %maximum_maximum_fusion.taps, bf16[768,768]{1,0:T(8,128)(2,1)} %wout.1, ...), custom_call_target="tpu_custom_call" | custom-call | flops 10000000000 | bytes 10000000 | tf_op jit(solution)/shard_map/pallas_call | solution.py:539
  117.3 0.0 copy-start
  117.3 0.0 copy-start.1
  117.3 0.9 slice_add_fusion
  118.3 0.6 slice.17
  118.8 0.6 copy.15
  119.5 2.1 %copy.20 = bf16[1,1,512,768]{3,2,1,0:T(8,128)(2,1)} copy(bf16[1,1,512,768]{3,2,1,0:T(8,128)(2,1)} %bitcast.10) | data formatting | bytes 1572864
  121.5 2.1 %copy.21 = bf16[1,1,512,768]{3,2,1,0:T(8,128)(2,1)} copy(bf16[1,1,512,768]{3,2,1,0:T(8,128)(2,1)} %bitcast.9) | data formatting | bytes 1572864
  123.6 0.0 copy-done
  123.6 0.9 copy.22
  124.5 0.0 copy-done.1
  124.5 0.7 copy.23
Async XLA Ops:
  117.3 6.3 %copy-start = (f32[96,2304]{1,0:T(8,128)S(1)}, f32[96,2304]{1,0:T(8,128)}, u32[]{:S(2)}) copy-start(f32[96,2304]{1,0:T(8,128)} %get-tuple-element.30) | copy-start | bytes 2654212
  117.3 7.2 %copy-start.1 = (f32[96,768]{1,0:T(8,128)S(1)}, f32[96,768]{1,0:T(8,128)}, u32[]{:S(2)}) copy-start(f32[96,768]{1,0:T(8,128)} %get-tuple-element.31) | copy-start | bytes 884740
